TPU v7x, 256 devices: a whole 4x4x8 slice. The times are simulated.
256 devices in a mesh: clus: 16 (over y_hi, x, core), rep: 16 (over y_lo, z).
Axes of the slice: x: 4, y: 4 (y_hi: 2, y_lo: 2; y = y_hi * 2 + y_lo), z: 8, core: 2. Of those that a mesh axis runs over, the one named last changes fastest.
Arguments:
- embeddings: bfloat16 [65536, 768], P(('clus', 'rep')), may hold values from -6 to 6
- assignment: int32 [65536, 1], P(('clus', 'rep')), may hold values from 0 to 47; in each aligned block of 256 rows (0 to 255, 256 to 511, ...) at most 16 rows name the same one
- ordering: int32 [65536], P(('clus', 'rep')), may hold values from 0 to 65535, each once
Outputs:
- nearest: float32 [65536], P(('clus', 'rep'))
Inputs may be any that keep to these rules, and one draw needn't show every extreme that they name: `assignment`: among the rows of one device (aligned blocks of 256 rows) no cluster is named more than 16 times, a bound that some block reaches. `ordering`: each position occurs once.
All inputs are finite; a program needn't handle non-finite values.
Results may differ from a plain program's by a relative error of at most 0.0014.
Values may be sent and summed in bfloat16 or wider, within the bound.
A program may use at most 64 MiB of HBM per device.

v0:
```python
import math

import jax
import jax.numpy as jnp
from jax import lax
from jax.sharding import PartitionSpec as P

CPO = 3


vacant_key = 1073741824


def as_sent(value):
    return jax.tree.map(lambda a: a.astype(jnp.bfloat16) if a.dtype == jnp.float32 else a, value)


def unit_rows(embeddings):
    widened = embeddings.astype(jnp.float32)
    scale = lax.rsqrt(jnp.sum(widened * widened, axis=1, keepdims=True) + 1e-06)
    return (widened * scale).astype(jnp.bfloat16)


def tile_scores(query_units, key_units):
    return jnp.einsum("kqd,kmd->kqm", query_units, key_units, preferred_element_type=jnp.float32)


def on_device(embeddings, assignment, ordering):
    clus_count = lax.axis_size("clus")
    row_count = embeddings.shape[0]
    features = embeddings.shape[1]
    per_cluster = row_count // 16
    cluster_count = CPO * clus_count
    slot_count = cluster_count * per_cluster
    group_span = clus_count * per_cluster
    normed = unit_rows(embeddings)
    row_cluster = assignment[:, 0]
    member_hot = (
        row_cluster[:, None] == jnp.arange(cluster_count, dtype=jnp.int32)[None, :]
    ).astype(jnp.int32)
    before = jnp.cumsum(member_hot, axis=0) - member_hot
    position = jnp.sum(before * member_hot, axis=1)
    slot_of = row_cluster * per_cluster + position
    placing = slot_of[None, :] == jnp.arange(slot_count, dtype=jnp.int32)[:, None]
    packed = jnp.dot(
        placing.astype(jnp.bfloat16), normed, preferred_element_type=jnp.float32
    ).astype(jnp.bfloat16)
    packed_keys = jnp.min(jnp.where(placing, ordering[None, :], vacant_key), axis=1)
    send_units = packed.reshape(clus_count, CPO, per_cluster, features)
    send_keys = packed_keys.reshape(clus_count, CPO, per_cluster)
    got_units, got_keys = (
        lax.all_to_all(send_units, "clus", split_axis=0, concat_axis=2, tiled=True),
        lax.all_to_all(send_keys, "clus", split_axis=0, concat_axis=2, tiled=True),
    )
    local_units = got_units.reshape(CPO, group_span, features)
    local_keys = got_keys.reshape(CPO, group_span)
    start_best = jnp.full((CPO, group_span), -1.0, jnp.float32)
    piece_units = lax.all_gather(local_units, "rep", axis=1, tiled=True)
    piece_keys = lax.all_gather(as_sent(local_keys), "rep", axis=1, tiled=True)
    piece_rows = piece_units.shape[1]
    stride = math.gcd(piece_rows, 256)

    def one_block(block_index, current):
        block_units = lax.dynamic_slice_in_dim(piece_units, block_index * stride, stride, 1)
        block_keys = lax.dynamic_slice_in_dim(piece_keys, block_index * stride, stride, 1)
        scores = tile_scores(local_units, block_units)
        earlier = block_keys[:, None, :] < local_keys[:, :, None]
        return jnp.maximum(current, jnp.max(jnp.where(earlier, scores, -1.0), axis=2))

    nearest = lax.fori_loop(0, piece_rows // stride, one_block, start_best)
    answer = lax.all_to_all(
        nearest.reshape(1, CPO, group_span), "clus", split_axis=2, concat_axis=0, tiled=True
    )
    flattened = answer.reshape(slot_count)
    return jnp.take(flattened, slot_of)


def solution(mesh):
    in_specs = (P(("clus", "rep"), None), P(("clus", "rep"), None), P(("clus", "rep")))
    out_specs = P(("clus", "rep"))
    return jax.shard_map(
        on_device, mesh=mesh, in_specs=in_specs, out_specs=out_specs, check_vma=False
    )
```

profile of v0, /device:TPU:1, one launch (start us, length us, event | category | flops | bytes accessed | tf_op | source)
XLA Modules:
  0.0 300.5 jit_solution(10705416820647998608)
XLA Ops:
  12.2 27.1 %all_to_all.49 = bf16[16,3,16,768]{3,2,1,0:T(8,128)(2,1)S(1)} all-to-all(bf16[16,3,16,768]{3,2,1,0:T(8,128)(2,1)S(1)} %bitcast.58), channel_id=1, replica_groups=mesh['clus'=16,'rep'=16] {'clus'}, dimensions={0} | all-to-all | bytes 2359296 | tf_op jit(solution)/shard_map/all_to_all | solution.py:52
  42.0 3.7 %all-to-all-start = ((s32[16,3,16]{2,1,0:T(4,128)}), s32[16,3,16]{2,1,0:T(4,128)S(1)}, u32[]{:S(2)}, u32[]{:S(2)}) async-start(s32[16,3,16]{2,1,0:T(4,128)} %reshape.61), calls=%async_computation | async-start | bytes 65536 | tf_op jit(solution)/shard_map/all_to_all | solution.py:53
  45.7 7.3 %all-to-all-done = s32[16,3,16]{2,1,0:T(4,128)S(1)} async-done(((s32[16,3,16]{2,1,0:T(4,128)}), s32[16,3,16]{2,1,0:T(4,128)S(1)}, u32[]{:S(2)}, u32[]{:S(2)}) %all-to-all-start) | async-done | bytes 3104 | tf_op jit(solution)/shard_map/all_to_all | solution.py:53
  53.2 32.3 %all_gather.6 = s32[3,4096]{1,0:T(4,128)S(1)} all-gather(s32[3,256]{1,0:T(4,128)S(1)} %reshape.62), channel_id=1, replica_groups=mesh['clus'=16,'rep'=16] {'rep'}, dimensions={1}, use_global_device_ids=true | all-gather | bytes 52224 | tf_op jit(solution)/shard_map/all_gather | solution.py:59
  85.5 160.6 %all-gather.2.cloned.1.call-done = bf16[3,4096,768]{2,1,0:T(8,128)(2,1)} async-done(((bf16[3,256,768]{2,1,0:T(8,128)(2,1)}), bf16[3,4096,768]{2,1,0:T(8,128)(2,1)}) %all-gather.2.cloned.1.call-update) | async-done | bytes 18874384 | tf_op jit(solution)/shard_map/all_gather | solution.py:58
  246.1 29.8 %while.14 = (s32[]{:T(128)}, f32[3,256]{1,0:T(4,128)S(1)}, s32[3,4096]{1,0:T(4,128)S(1)}, s32[1,3,256]{2,1,0:T(4,128)S(1)}, bf16[3,4096,768]{2,1,0:T(8,128)(2,1)...) while((s32[]{:T(128)}, f32[3,256]{1,0:T(4,128)S(1)}, ...), condition=%wide.region_7.8_spmd.clone, body=%wide.region_5.7_spmd.clone.sunk | while | flops 302580480 | bytes 2384045 | solution.py:70
  246.1 1.8 fusion.19
  247.9 1.8 fusion.19
  249.8 1.8 fusion.19
  251.7 1.8 fusion.19
  253.5 1.8 fusion.19
  255.4 1.8 fusion.19
  257.2 1.8 fusion.19
  259.1 1.8 fusion.19
  261.0 1.8 fusion.19
  262.8 1.8 fusion.19
  264.7 1.8 fusion.19
  266.6 1.8 fusion.19
  268.4 1.8 fusion.19
  270.3 1.8 fusion.19
  272.2 1.8 fusion.19
  274.0 1.8 fusion.19
  276.6 7.2 %all-to-all-start.2 = ((f32[1,3,256]{1,0,2:T(1,128)}), f32[1,3,256]{1,0,2:T(1,128)S(1)}, u32[]{:S(2)}, u32[]{:S(2)}) async-start(f32[1,3,256]{1,0,2:T(1,128)} %bitcast.11), calls=%async_computation.2 | async-start | bytes 262144 | tf_op jit(solution)/shard_map/all_to_all | solution.py:71
  283.8 7.6 %all-to-all-done.2 = f32[1,3,256]{1,0,2:T(1,128)S(1)} async-done(((f32[1,3,256]{1,0,2:T(1,128)}), f32[1,3,256]{1,0,2:T(1,128)S(1)}, u32[]{:S(2)}, u32[]{:S(2)}) %all-to-all-start.2) | async-done | bytes 3104 | tf_op jit(solution)/shard_map/all_to_all | solution.py:71
  (66 shorter events, 11.9 us)
Async XLA Ops:
  6.5 239.5 %all-gather.2.cloned.1.call-start = ((), (), s32[]{:S(2)}) async-start(), calls=%async_computation.3 | async-start | bytes 20054016 | tf_op jit(solution)/shard_map/all_gather | solution.py:58
  40.4 0.7 copy-start.2
  40.4 5.2 %copy-start.1 = (s32[256,1]{0,1:T(1,128)S(1)}, s32[256,1]{0,1:T(1,128)}, u32[]{:S(2)}) copy-start(s32[256,1]{0,1:T(1,128)} %param.6) | copy-start | bytes 3076
  40.4 205.6 %copy-start = (bf16[1,3,16,16,768]{4,3,2,1,0:T(8,128)(2,1)S(1)}, bf16[1,3,16,16,768]{4,3,2,1,0:T(8,128)(2,1)}, u32[]{:S(2)}) copy-start(bf16[1,3,16,16,768]{4,3,2,1,0:T(8,128)(2,1)} %copy.27) | copy-start | bytes 3538948
  42.0 11.1 %all-to-all-start = ((s32[16,3,16]{2,1,0:T(4,128)}), s32[16,3,16]{2,1,0:T(4,128)S(1)}, u32[]{:S(2)}, u32[]{:S(2)}) async-start(s32[16,3,16]{2,1,0:T(4,128)} %reshape.61), calls=%async_computation | async-start | bytes 65536 | tf_op jit(solution)/shard_map/all_to_all | solution.py:53
  276.6 14.7 %all-to-all-start.2 = ((f32[1,3,256]{1,0,2:T(1,128)}), f32[1,3,256]{1,0,2:T(1,128)S(1)}, u32[]{:S(2)}, u32[]{:S(2)}) async-start(f32[1,3,256]{1,0,2:T(1,128)} %bitcast.11), calls=%async_computation.2 | async-start | bytes 262144 | tf_op jit(solution)/shard_map/all_to_all | solution.py:71
Sparse Core Ops, SparseCore 0:
  40.6 205.4 all-gather.1
where the time goes:
time: 301 us; the launch traced here: 300 us
  waiting for transfers between devices  176 us (58%)
  blocking collectives  59.3 us (20%)
  matrix products  30.4 us (10%)
  between operations  13.5 us (4%)
  starting transfers between devices  10.8 us (4%)
  local copies, waits for them, and re-layouts  5.38 us (2%)
  other arithmetic  4.91 us (2%)
    all_gather x1, waiting for transfers between devices, on_device(): piece_units = lax.all_gather(local_units, 'rep', axis=1, tiled=True)  161 us
    all_gather x1, blocking collectives, on_device(): piece_keys = lax.all_gather(as_sent(local_keys), 'rep', axis=1, tiled=True)  32.3 us
    dot_general x16, matrix products, tile_scores(): jnp.einsum('kqd,kmd->kqm', query_units, key_units, preferred_element_type...  28.9 us
    all_to_all x1, blocking collectives, on_device(): lax.all_to_all(send_units, 'clus', split_axis=0, concat_axis=2, tiled=True)  27.1 us
    all_to_all x1, waiting for transfers between devices, on_device(): lax.all_to_all(nearest.reshape(1, CPO, group_span), 'clus', split_axis=2,...  7.58 us
    all_to_all x1, waiting for transfers between devices, on_device(): lax.all_to_all(send_keys, 'clus', split_axis=0, concat_axis=2, tiled=True)  7.34 us
    all_to_all x1, starting transfers between devices, on_device(): lax.all_to_all(nearest.reshape(1, CPO, group_span), 'clus', split_axis=2,...  7.16 us
  transfers between devices with their start and end apart: 3, of which 3 were waited for; matrix products, arithmetic and copies ran while one was open for 0% of the time, Pallas kernels for 0%

commit v1 on v0

v1 whole, which is shorter than its diff:
```python
import jax
import jax.numpy as jnp
from jax import lax
from jax.experimental import pallas as pl
from jax.experimental.pallas import tpu as pltpu
from jax.sharding import PartitionSpec as P

PLANE = ((0, 0), (1, 0), (0, 1), (3, 3), (2, 0), (0, 2), (3, 2), (2, 3), (2, 2), (1, 3))
LINES = (0, 1, 7, 2, 6, 3, 5, 4)
SOURCE = (None, 0, 0, 0, 1, 2, 3, 3, 6, 1)
LANDS = (None, 0, 0, 0, 2, 2, 2, 2, 4, 4)
ONE_WAY = (1, 2, 3, 6, 7, 9)
UNITS = (
    [(0, 0)],
    [(1, 0)],
    [(r, g) for r in (0, 1, 2) for g in (1, 2, 3)],
    [(3, g) for g in range(4)] + [(4, g) for g in (1, 2, 3)],
    [(r, g) for r in (0, 1, 3) for g in (4, 5, 6, 7)] + [(r, g) for r in (2, 4) for g in (6, 7)],
    [(5, g) for g in range(8)] + [(6, g) for g in (1, 2, 3, 6, 7)],
    [(r, g) for r in (0, 1, 3, 5) for g in (8, 9)] + [(r, 9) for r in (2, 4, 6)] + [(7, g) for g in range(10)],
)
STEPS = len(UNITS)
MESH = pl.DeviceIdType.MESH
LOWEST = -(2**31)
SPAN = 65536


def whereabouts():
    clus, rep = lax.axis_index("clus"), lax.axis_index("rep")
    return (clus // 2) % 4, (clus // 8) * 2 + rep // 8, rep % 8, clus % 2


def relative(dx, dy, dz, other):
    x, y, z, core = whereabouts()
    x, y, z, core = (x + dx) % 4, (y + dy) % 4, (z + dz) % 8, (core + other) % 2
    return ((y // 2) * 4 + x) * 2 + core, (y % 2) * 8 + z


def pick(table, n):
    value = jnp.int32(table[0])
    for i in range(1, len(table)):
        value = jnp.where(n == i, jnp.int32(table[i]), value)
    return value


def scores(lines, r, columns, c):
    return lax.dot_general(
        lines[r], columns[c], (((1,), (1,)), ((), ())), preferred_element_type=jnp.float32
    )


def keep_best(s, r, c, column_labels, line_place, line_order, line_best, column_best):
    label = column_labels[c]
    wide = []
    for left in (0, 128):
        p = label[:, left : left + 128]
        wide.append(
            [
                jnp.broadcast_to(p + (LOWEST + 1), (8, 128)),
                jnp.broadcast_to(p + LOWEST - 1, (8, 128)),
                jnp.broadcast_to((p & (SPAN - 1)) + LOWEST, (8, 128)),
                jnp.full((8, 128), -1.0, jnp.float32),
            ]
        )
    for top in range(0, 256, 8):
        mine, order = line_place[r, top : top + 8, :], line_order[r, top : top + 8, :]
        best = line_best[r, top : top + 8, :]
        for i, left in enumerate((0, 128)):
            after, before, other_order, down = wide[i]
            v = s[top : top + 8, left : left + 128]
            best = jnp.maximum(best, jnp.where(mine - after < order, v, -1.0))
            wide[i][3] = jnp.maximum(down, jnp.where(before - mine < other_order, v, -1.0))
        line_best[r, top : top + 8, :] = best
    for i, left in enumerate((0, 128)):
        here = column_best.at[c, :, pl.ds(left, 128)]
        here[...] = jnp.maximum(here[...], wide[i][3])


def kernel(
    rows_ref, cluster_ref, order_ref, out_ref,
    lines, columns, line_labels, column_labels, line_place, line_order, line_best, column_best, even, odd,
    line_answers, same_answers, other_answers, sibling_in, line_got, column_got,
    up_sent, up_got, down_sent, down_got, line_label_sent, line_label_got,
    plane_sent, plane_got, plane_label_sent, plane_label_got,
    across_sent, across_got, across_label_sent, across_label_got,
    line_answer_sent, line_answer_got, plane_answer_sent, plane_answer_got, sibling_sent, sibling_got,
):
    def remote(src, dst, sent, got, device):
        return pltpu.make_async_remote_copy(src, dst, sent, got, device_id=device, device_id_type=MESH)

    barrier = pltpu.get_barrier_semaphore()
    hello = {(0, 0, 1, 0), (0, 0, 7, 0), (0, 0, 0, 1)}
    for k in range(1, len(PLANE)):
        (x, y), (a, b) = PLANE[k], PLANE[SOURCE[k]]
        hello.add(((x - a) % 4, (y - b) % 4, 0, 0))
    for offset in sorted(hello):
        pl.semaphore_signal(barrier, inc=1, device_id=relative(*offset), device_id_type=MESH)

    for top in range(0, 256, 32):
        wide = rows_ref[top : top + 32, :].astype(jnp.float32)
        scale = lax.rsqrt(jnp.sum(wide * wide, axis=1, keepdims=True) + 1e-06)
        unit = (wide * scale).astype(jnp.bfloat16)
        lines[0, top : top + 32, :] = unit
        columns[0, top : top + 32, :] = unit
    place = cluster_ref[...] * SPAN + order_ref[...]
    line_labels[0] = place
    column_labels[0] = place
    pl.semaphore_wait(barrier, len(hello))

    def half(ref, slot, h):
        return ref.at[slot, pl.ds(pl.multiple_of(h * 128, 128), 128)]

    def up(n):
        k, h = n // 2, n % 2
        source = jnp.maximum(2 * k - 1, 0)
        return remote(half(lines, source, h), half(lines, 2 * k + 1, h), up_sent.at[n], up_got.at[n], relative(0, 0, 7, 0))

    def down(n):
        k, h = n // 2, 1 - n % 2
        return remote(
            half(lines, 2 * k, h), half(lines, jnp.minimum(2 * k + 2, 7), h),
            down_sent.at[n], down_got.at[n], relative(0, 0, 1, 0),
        )

    def up_label(k):
        source = jnp.maximum(2 * k - 1, 0)
        i = 2 * k + 1
        return remote(line_labels.at[source], line_labels.at[i], line_label_sent.at[i], line_label_got.at[i], relative(0, 0, 7, 0))

    def down_label(k):
        i = 2 * k + 2
        return remote(line_labels.at[2 * k], line_labels.at[i], line_label_sent.at[i], line_label_got.at[i], relative(0, 0, 1, 0))

    def between(k):
        (x, y), (a, b) = PLANE[k], PLANE[SOURCE[k]]
        return relative((a - x) % 4, (b - y) % 4, 0, 0)

    def plane(k, h):
        return remote(
            half(columns, 2 * SOURCE[k], h), half(columns, 2 * k, h),
            plane_sent.at[k, h], plane_got.at[k, h], between(k),
        )

    def plane_label(k):
        return remote(
            column_labels.at[2 * SOURCE[k]], column_labels.at[2 * k],
            plane_label_sent.at[k], plane_label_got.at[k], between(k),
        )

    def across(k):
        return remote(
            columns.at[2 * k], columns.at[2 * k + 1], across_sent.at[k], across_got.at[k], relative(0, 0, 0, 1)
        )

    def across_label(k):
        return remote(
            column_labels.at[2 * k], column_labels.at[2 * k + 1],
            across_label_sent.at[k], across_label_got.at[k], relative(0, 0, 0, 1),
        )

    first = [k for k in range(1, len(PLANE)) if LANDS[k] == 0]
    for h in (0, 1):
        up(jnp.int32(h)).start()
        down(jnp.int32(h)).start()
        for k in first:
            plane(k, h).start()
        if h == 0:
            up_label(jnp.int32(0)).start()
            down_label(jnp.int32(0)).start()
            for k in first:
                plane_label(k).start()
    across(0).start()
    across_label(0).start()

    line_best[...] = jnp.full(line_best.shape, -1.0, jnp.float32)
    column_best[...] = jnp.full(column_best.shape, -1.0, jnp.float32)
    odd[...] = jnp.full(odd.shape, -1.0, jnp.float32)

    def spread(r):
        for top in (0, 128):
            column = jnp.broadcast_to(line_labels[r, :, top : top + 128], (128, 128)).T
            line_place[r, top : top + 128, :] = column
            line_order[r, top : top + 128, :] = (column & (SPAN - 1)) + LOWEST

    spread(0)

    flat = [u for step in UNITS for u in step]
    starts = [sum(len(s) for s in UNITS[:n]) for n in range(STEPS + 1)]
    words = []
    for i in range(0, len(flat), 4):
        words.append(sum((r * 16 + g) << (7 * j) for j, (r, g) in enumerate(flat[i : i + 4])))

    def step(n, before):
        k, h = n // 2, n % 2
        up(n).wait_recv()
        down(n).wait_recv()

        @pl.when(n < STEPS - 2)
        def _():
            up(n + 2).start()
            down(n + 2).start()

        @pl.when(h == 0)
        def _():
            up_label(k).wait_recv()

            @pl.when(k < 3)
            def _():
                up_label(k + 1).start()
                down_label(k).wait_recv()

            @pl.when(k < 2)
            def _():
                down_label(k + 1).start()

        for at in (0, 2, 4):
            landing = [j for j in range(1, len(PLANE)) if LANDS[j] == at]

            @pl.when((n == at) | (n == at + 1))
            def _():
                for j in landing:
                    plane(j, h).wait_recv()
                for j in range(1, len(PLANE)):
                    if LANDS[j] == at + 2:
                        plane(j, h).start()

            @pl.when(n == at)
            def _():
                for j in landing:
                    plane_label(j).wait_recv()
                for j in range(1, len(PLANE)):
                    if LANDS[j] == at + 2:
                        plane_label(j).start()
                for j in [0] if at == 0 else [j for j in range(1, len(PLANE)) if LANDS[j] == at - 2]:
                    across(j).wait_recv()
                    across_label(j).wait_recv()

            @pl.when(n == at + 1)
            def _():
                for j in landing:
                    across(j).start()
                    across_label(j).start()

        @pl.when(n == 6)
        def _():
            for j in range(1, len(PLANE)):
                if LANDS[j] == 4:
                    across(j).wait_recv()
                    across_label(j).wait_recv()

            spread(7)

        @pl.when(h == 1)
        def _():
            spread(2 * k + 1)
            spread(2 * k + 2)

        def unit(u, carry):
            last_r, last_c = carry
            code = (pick(words, u // 4) >> ((u % 4) * 7)) & 127
            r, g = code >> 4, code & 15
            even[...] = scores(lines, r, columns, 2 * g)
            keep_best(odd, last_r, last_c, column_labels, line_place, line_order, line_best, column_best)
            odd[...] = scores(lines, r, columns, 2 * g + 1)
            keep_best(even, r, 2 * g, column_labels, line_place, line_order, line_best, column_best)
            return r, 2 * g + 1

        return lax.fori_loop(pick(starts, n), pick(starts[1:], n), unit, before)

    last_r, last_c = lax.fori_loop(0, STEPS, step, (jnp.int32(0), jnp.int32(0)))
    keep_best(odd, last_r, last_c, column_labels, line_place, line_order, line_best, column_best)

    def column_best_of(c):
        return jnp.max(column_best[c], axis=0, keepdims=True)

    for g in range(len(PLANE)):
        other_answers[g] = column_best_of(2 * g + 1)
    to_sibling = remote(other_answers, sibling_in, sibling_sent, sibling_got, relative(0, 0, 0, 1))
    to_sibling.start()

    def line_answer(r):
        return remote(
            line_answers.at[r], line_got.at[r], line_answer_sent.at[r], line_answer_got.at[r],
            relative(0, 0, LINES[r], 0),
        )

    def plane_answer(g):
        return remote(
            same_answers.at[g], column_got.at[g], plane_answer_sent.at[g], plane_answer_got.at[g],
            relative(*PLANE[g], 0, 0),
        )

    for r in range(8):
        line_answers[r] = jnp.max(line_best[r].T, axis=0, keepdims=True)
        if r:
            line_answer(r).start()
    to_sibling.wait_recv()
    for g in range(len(PLANE)):
        same_answers[g] = jnp.maximum(column_best_of(2 * g), sibling_in[g])
        if g:
            plane_answer(g).start()
    best = jnp.maximum(line_answers[0], same_answers[0])
    for r in range(1, 8):
        line_answer(r).wait_recv()
        best = jnp.maximum(best, line_got[r])
    for g in range(1, len(PLANE)):
        plane_answer(g).wait_recv()
        best = jnp.maximum(best, column_got[g])
    out_ref[...] = best

    to_sibling.wait_send()
    for r in range(1, 8):
        line_answer(r).wait_send()
    for g in range(1, len(PLANE)):
        plane_answer(g).wait_send()
        plane_label(g).wait_send()
        for h in (0, 1):
            plane(g, h).wait_send()
    for g in range(len(PLANE)):
        across(g).wait_send()
        across_label(g).wait_send()
    for n in range(STEPS):
        up(jnp.int32(n)).wait_send()
        down(jnp.int32(n)).wait_send()
    for k in range(4):
        up_label(jnp.int32(k)).wait_send()
    for k in range(3):
        down_label(jnp.int32(k)).wait_send()


def on_device(embeddings, assignment, ordering):
    rows, features = embeddings.shape
    plane = len(PLANE)
    dma = pltpu.SemaphoreType.DMA
    best = pl.pallas_call(
        kernel,
        out_shape=jax.ShapeDtypeStruct((1, rows), jnp.float32),
        in_specs=[pl.BlockSpec(memory_space=pltpu.VMEM)] * 3,
        out_specs=pl.BlockSpec(memory_space=pltpu.VMEM),
        scratch_shapes=[
            pltpu.VMEM((8, rows, features), jnp.bfloat16),
            pltpu.VMEM((2 * plane, rows, features), jnp.bfloat16),
            pltpu.VMEM((8, 1, rows), jnp.int32),
            pltpu.VMEM((2 * plane, 1, rows), jnp.int32),
            pltpu.VMEM((8, rows, 128), jnp.int32),
            pltpu.VMEM((8, rows, 128), jnp.int32),
            pltpu.VMEM((8, rows, 128), jnp.float32),
            pltpu.VMEM((2 * plane, 8, rows), jnp.float32),
            pltpu.VMEM((rows, rows), jnp.float32),
            pltpu.VMEM((rows, rows), jnp.float32),
            pltpu.VMEM((8, 1, rows), jnp.float32),
            pltpu.VMEM((plane, 1, rows), jnp.float32),
            pltpu.VMEM((plane, 1, rows), jnp.float32),
            pltpu.VMEM((plane, 1, rows), jnp.float32),
            pltpu.VMEM((8, 1, rows), jnp.float32),
            pltpu.VMEM((plane, 1, rows), jnp.float32),
            *[dma((STEPS,))] * 4,
            *[dma((8,))] * 2,
            *[dma((plane, 2))] * 2,
            *[dma((plane,))] * 2,
            *[dma((plane,))] * 4,
            *[dma((8,))] * 2,
            *[dma((plane,))] * 2,
            *[dma(())] * 2,
        ],
        compiler_params=pltpu.CompilerParams(
            collective_id=0, has_side_effects=True, vmem_limit_bytes=48 * 2**20
        ),
        cost_estimate=pl.CostEstimate(
            flops=2 * 136 * rows * rows * features, bytes_accessed=rows * features * 2, transcendentals=rows
        ),
    )(embeddings, assignment.reshape(1, rows), ordering.reshape(1, rows))
    return best.reshape(rows)


def solution(mesh):
    in_specs = (P(("clus", "rep"), None), P(("clus", "rep"), None), P(("clus", "rep")))
    out_specs = P(("clus", "rep"))
    return jax.shard_map(
        on_device, mesh=mesh, in_specs=in_specs, out_specs=out_specs, check_vma=False
    )
```

time: 301 us -> 66.7 us (0.22)
  waiting for transfers between devices: 176 us -> 0 us
  Pallas kernels: 0 us -> 64.3 us
  blocking collectives: 59.3 us -> 0 us
  matrix products: 30.4 us -> 0 us
  between operations: 13.5 us -> 0.01 us
  starting transfers between devices: 10.8 us -> 0 us
  other arithmetic: 4.91 us -> 0 us
  local copies, waits for them, and re-layouts: 5.38 us -> 2.25 us
    all_gather x1 -> x0, waiting for transfers between devices: 161 us -> none  [on_device(): piece_units = lax.all_gather(local_units, 'rep', axis=1, tiled=True)]
    pallas_call x0 -> x1, Pallas kernels: none -> 64.3 us  [on_device(): pl.pallas_call(kernel, out_shape=jax.ShapeDtypeStruct((1, rows), jnp.floa...]
    all_gather x1 -> x0, blocking collectives: 32.3 us -> none  [on_device(): piece_keys = lax.all_gather(as_sent(local_keys), 'rep', axis=1, tiled=True)]
    dot_general x17 -> x0, matrix products: 30.4 us -> none  [the longest x16 28.9 us: tile_scores(): jnp.einsum('kqd,kmd->kqm', query_units, key_units, preferred_element_type...]
    all_to_all x1 -> x0, blocking collectives: 27.1 us -> none  [on_device(): lax.all_to_all(send_units, 'clus', split_axis=0, concat_axis=2, tiled=True)]
    all_to_all x2 -> x0, waiting for transfers between devices: 14.9 us -> none  [the longest x1 7.58 us: on_device(): lax.all_to_all(nearest.reshape(1, CPO, group_span), 'clus', split_axis=2,...]
    all_to_all x2 -> x0, starting transfers between devices: 10.8 us -> none  [the longest x1 7.16 us: on_device(): lax.all_to_all(nearest.reshape(1, CPO, group_span), 'clus', split_axis=2,...]
  transfers between devices with their start and end apart: 3 -> 0, of which waited for: 3 -> 0; matrix products, arithmetic and copies ran while one was open for 0% -> 0% of each run, Pallas kernels for 0% -> 0%
where the time goes in v1:
time: 66.7 us; the launch traced here: 66.6 us
  Pallas kernels  64.3 us (96%)
  local copies, waits for them, and re-layouts  2.25 us (3%)
    pallas_call x1, Pallas kernels, on_device(): pl.pallas_call(kernel, out_shape=jax.ShapeDtypeStruct((1, rows), jnp.floa...  64.3 us
    unnamed x7, local copies, waits for them, and re-layouts  2.25 us

profile of v1, /device:TPU:1, one launch (start us, length us, event | category | flops | bytes accessed | tf_op | source)
XLA Modules:
  0.0 66.6 jit_solution(2186701591645963732)
XLA Ops:
  0.0 0.0 copy-start.2
  0.0 0.0 copy-start.1
  0.0 0.7 %copy-done.2 = s32[256]{0:T(256)S(1)} copy-done((s32[256]{0:T(256)S(1)}, s32[256]{0:T(256)}, u32[]{:S(2)}) %copy-start.2) | copy-done | bytes 1048
  0.7 0.0 copy-done.1
  0.7 0.0 copy-start
  0.7 1.0 %copy-done = bf16[256,768]{1,0:T(8,128)(2,1)S(1)} copy-done((bf16[256,768]{1,0:T(8,128)(2,1)S(1)}, bf16[256,768]{1,0:T(8,128)(2,1)}, u32[]{:S(2)}) %copy-start) | copy-done | bytes 393240
  1.7 64.3 %shard_map.37 = f32[1,256]{1,0:T(1,128)S(1)} custom-call(bf16[256,768]{1,0:T(8,128)(2,1)S(1)} %copy-done, s32[1,256]{1,0:T(1,128)S(1)} %bitcast.4, s32[1,256]{1,0:T(1,128)S(1)} %bitcast.5), custom_call_target="tpu_custom_call" | custom-call | flops 13690208256 | bytes 393216 | tf_op jit(solution)/shard_map/pallas_call | solution.py:335
  66.0 0.6 copy.5
Async XLA Ops:
  0.0 0.7 %copy-start.2 = (s32[256]{0:T(256)S(1)}, s32[256]{0:T(256)}, u32[]{:S(2)}) copy-start(s32[256]{0:T(256)} %param.5) | copy-start | bytes 3076
  0.0 0.7 %copy-start.1 = (s32[256,1]{0,1:T(1,128)S(1)}, s32[256,1]{0,1:T(1,128)}, u32[]{:S(2)}) copy-start(s32[256,1]{0,1:T(1,128)} %param.4) | copy-start | bytes 3076
  0.7 1.0 %copy-start = (bf16[256,768]{1,0:T(8,128)(2,1)S(1)}, bf16[256,768]{1,0:T(8,128)(2,1)}, u32[]{:S(2)}) copy-start(bf16[256,768]{1,0:T(8,128)(2,1)} %rows_ref.1) | copy-start | bytes 1179652

commit v2 on v1

--- a/solution.py
+++ b/solution.py
@@ -9,15 +9,16 @@
 LINES = (0, 1, 7, 2, 6, 3, 5, 4)
 SOURCE = (None, 0, 0, 0, 1, 2, 3, 3, 6, 1)
 LANDS = (None, 0, 0, 0, 2, 2, 2, 2, 4, 4)
-ONE_WAY = (1, 2, 3, 6, 7, 9)
+GROUP = 4
 UNITS = (
-    [(0, 0)],
-    [(1, 0)],
-    [(r, g) for r in (0, 1, 2) for g in (1, 2, 3)],
-    [(3, g) for g in range(4)] + [(4, g) for g in (1, 2, 3)],
-    [(r, g) for r in (0, 1, 3) for g in (4, 5, 6, 7)] + [(r, g) for r in (2, 4) for g in (6, 7)],
-    [(5, g) for g in range(8)] + [(6, g) for g in (1, 2, 3, 6, 7)],
-    [(r, g) for r in (0, 1, 3, 5) for g in (8, 9)] + [(r, 9) for r in (2, 4, 6)] + [(7, g) for g in range(10)],
+    [],
+    [],
+    [(r, g) for r in (0, 1) for g in range(4)],
+    [(2, g) for g in (1, 2, 3)] + [(3, g) for g in range(4)] + [(4, 1)],
+    [(4, 2), (4, 3)] + [(r, g) for r in (0, 1, 3) for g in (4, 5, 6, 7)] + [(2, 6), (2, 7)],
+    [(4, 6), (4, 7)] + [(5, g) for g in range(8)] + [(6, 1), (6, 2)],
+    [(6, 3), (6, 6), (6, 7)] + [(r, g) for r in (0, 1, 3, 5) for g in (8, 9)] + [(r, 9) for r in (2, 4, 6)]
+    + [(7, g) for g in range(10)],
 )
 STEPS = len(UNITS)
 MESH = pl.DeviceIdType.MESH
@@ -185,10 +186,10 @@
     spread(0)
 
     flat = [u for step in UNITS for u in step]
-    starts = [sum(len(s) for s in UNITS[:n]) for n in range(STEPS + 1)]
+    starts = [sum(len(s) for s in UNITS[:n]) // GROUP for n in range(STEPS + 1)]
     words = []
-    for i in range(0, len(flat), 4):
-        words.append(sum((r * 16 + g) << (7 * j) for j, (r, g) in enumerate(flat[i : i + 4])))
+    for i in range(0, len(flat), GROUP):
+        words.append(sum((r * 16 + g) << (7 * j) for j, (r, g) in enumerate(flat[i : i + GROUP])))
 
     def step(n, before):
         k, h = n // 2, n % 2
@@ -255,17 +256,20 @@
             spread(2 * k + 1)
             spread(2 * k + 2)
 
-        def unit(u, carry):
+        def group(u, carry):
             last_r, last_c = carry
-            code = (pick(words, u // 4) >> ((u % 4) * 7)) & 127
-            r, g = code >> 4, code & 15
-            even[...] = scores(lines, r, columns, 2 * g)
-            keep_best(odd, last_r, last_c, column_labels, line_place, line_order, line_best, column_best)
-            odd[...] = scores(lines, r, columns, 2 * g + 1)
-            keep_best(even, r, 2 * g, column_labels, line_place, line_order, line_best, column_best)
-            return r, 2 * g + 1
-
-        return lax.fori_loop(pick(starts, n), pick(starts[1:], n), unit, before)
+            word = pick(words, u)
+            for i in range(GROUP):
+                code = (word >> (7 * i)) & 127
+                r, g = code >> 4, code & 15
+                even[...] = scores(lines, r, columns, 2 * g)
+                keep_best(odd, last_r, last_c, column_labels, line_place, line_order, line_best, column_best)
+                odd[...] = scores(lines, r, columns, 2 * g + 1)
+                keep_best(even, r, 2 * g, column_labels, line_place, line_order, line_best, column_best)
+                last_r, last_c = r, 2 * g + 1
+            return last_r, last_c
+
+        return lax.fori_loop(pick(starts, n), pick(starts[1:], n), group, before)
 
     last_r, last_c = lax.fori_loop(0, STEPS, step, (jnp.int32(0), jnp.int32(0)))
     keep_best(odd, last_r, last_c, column_labels, line_place, line_order, line_best, column_best)

time: 66.7 us -> 60.6 us (0.909)
  Pallas kernels: 64.3 us -> 58.2 us
    pallas_call x1, Pallas kernels: 64.3 us -> 58.2 us  [on_device(): pl.pallas_call(kernel, out_shape=jax.ShapeDtypeStruct((1, rows), jnp.floa...]
where the time goes in v2:
time: 60.6 us; the launch traced here: 60.5 us
  Pallas kernels  58.2 us (96%)
  local copies, waits for them, and re-layouts  2.25 us (4%)
    pallas_call x1, Pallas kernels, on_device(): pl.pallas_call(kernel, out_shape=jax.ShapeDtypeStruct((1, rows), jnp.floa...  58.2 us
    unnamed x7, local copies, waits for them, and re-layouts  2.25 us

profile of v2, /device:TPU:1, one launch (start us, length us, event | category | flops | bytes accessed | tf_op | source)
XLA Modules:
  0.0 60.5 jit_solution(12576050335199009083)
XLA Ops:
  0.0 0.0 copy-start.2
  0.0 0.0 copy-start.1
  0.0 0.7 %copy-done.2 = s32[256]{0:T(256)S(1)} copy-done((s32[256]{0:T(256)S(1)}, s32[256]{0:T(256)}, u32[]{:S(2)}) %copy-start.2) | copy-done | bytes 1048
  0.7 0.0 copy-done.1
  0.7 0.0 copy-start
  0.7 1.0 %copy-done = bf16[256,768]{1,0:T(8,128)(2,1)S(1)} copy-done((bf16[256,768]{1,0:T(8,128)(2,1)S(1)}, bf16[256,768]{1,0:T(8,128)(2,1)}, u32[]{:S(2)}) %copy-start) | copy-done | bytes 393240
  1.7 58.2 %shard_map.37 = f32[1,256]{1,0:T(1,128)S(1)} custom-call(bf16[256,768]{1,0:T(8,128)(2,1)S(1)} %copy-done, s32[1,256]{1,0:T(1,128)S(1)} %bitcast.4, s32[1,256]{1,0:T(1,128)S(1)} %bitcast.5), custom_call_target="tpu_custom_call" | custom-call | flops 13690208256 | bytes 393216 | tf_op jit(solution)/shard_map/pallas_call | solution.py:339
  59.9 0.6 copy.5
Async XLA Ops:
  0.0 0.7 %copy-start.2 = (s32[256]{0:T(256)S(1)}, s32[256]{0:T(256)}, u32[]{:S(2)}) copy-start(s32[256]{0:T(256)} %param.5) | copy-start | bytes 3076
  0.0 0.7 %copy-start.1 = (s32[256,1]{0,1:T(1,128)S(1)}, s32[256,1]{0,1:T(1,128)}, u32[]{:S(2)}) copy-start(s32[256,1]{0,1:T(1,128)} %param.4) | copy-start | bytes 3076
  0.7 1.0 %copy-start = (bf16[256,768]{1,0:T(8,128)(2,1)S(1)}, bf16[256,768]{1,0:T(8,128)(2,1)}, u32[]{:S(2)}) copy-start(bf16[256,768]{1,0:T(8,128)(2,1)} %rows_ref.1) | copy-start | bytes 1179652

commit v3 on v2

--- a/solution.py
+++ b/solution.py
@@ -11,14 +11,19 @@
 LANDS = (None, 0, 0, 0, 2, 2, 2, 2, 4, 4)
 GROUP = 4
 UNITS = (
-    [],
-    [],
-    [(r, g) for r in (0, 1) for g in range(4)],
-    [(2, g) for g in (1, 2, 3)] + [(3, g) for g in range(4)] + [(4, 1)],
-    [(4, 2), (4, 3)] + [(r, g) for r in (0, 1, 3) for g in (4, 5, 6, 7)] + [(2, 6), (2, 7)],
-    [(4, 6), (4, 7)] + [(5, g) for g in range(8)] + [(6, 1), (6, 2)],
-    [(6, 3), (6, 6), (6, 7)] + [(r, g) for r in (0, 1, 3, 5) for g in (8, 9)] + [(r, 9) for r in (2, 4, 6)]
-    + [(7, g) for g in range(10)],
+    ([], []),
+    ([], [(r, g) for r in (0, 1) for g in range(4)]),
+    ([], []),
+    (
+        [(2, g) for g in (1, 2, 3)] + [(3, g) for g in range(4)] + [(4, 1)],
+        [(4, 2), (4, 3), (2, 6), (2, 7)] + [(0, g) for g in (4, 5, 6, 7)],
+    ),
+    ([(r, g) for r in (1, 3) for g in (4, 5, 6, 7)], []),
+    (
+        [(4, 6), (4, 7)] + [(5, g) for g in range(8)] + [(6, 1), (6, 2)],
+        [(6, 3), (6, 6), (6, 7)] + [(r, g) for r in (0, 1, 3, 5) for g in (8, 9)] + [(2, 9)],
+    ),
+    ([(4, 9), (6, 9), (7, 0), (7, 1)], [(7, g) for g in range(2, 10)]),
 )
 STEPS = len(UNITS)
 MESH = pl.DeviceIdType.MESH
@@ -78,7 +83,7 @@
 
 
 def kernel(
-    rows_ref, cluster_ref, order_ref, out_ref,
+    rows_hbm, cluster_hbm, order_hbm, out_ref, rows_ref, cluster_ref, order_ref, loaded,
     lines, columns, line_labels, column_labels, line_place, line_order, line_best, column_best, even, odd,
     line_answers, same_answers, other_answers, sibling_in, line_got, column_got,
     up_sent, up_got, down_sent, down_got, line_label_sent, line_label_got,
@@ -89,6 +94,12 @@
     def remote(src, dst, sent, got, device):
         return pltpu.make_async_remote_copy(src, dst, sent, got, device_id=device, device_id_type=MESH)
 
+    loads = [
+        pltpu.make_async_copy(src, dst, loaded.at[i])
+        for i, (src, dst) in enumerate(((rows_hbm, rows_ref), (cluster_hbm, cluster_ref), (order_hbm, order_ref)))
+    ]
+    for load in loads:
+        load.start()
     barrier = pltpu.get_barrier_semaphore()
     hello = {(0, 0, 1, 0), (0, 0, 7, 0), (0, 0, 0, 1)}
     for k in range(1, len(PLANE)):
@@ -97,12 +108,15 @@
     for offset in sorted(hello):
         pl.semaphore_signal(barrier, inc=1, device_id=relative(*offset), device_id_type=MESH)
 
+    loads[0].wait()
     for top in range(0, 256, 32):
         wide = rows_ref[top : top + 32, :].astype(jnp.float32)
         scale = lax.rsqrt(jnp.sum(wide * wide, axis=1, keepdims=True) + 1e-06)
         unit = (wide * scale).astype(jnp.bfloat16)
         lines[0, top : top + 32, :] = unit
         columns[0, top : top + 32, :] = unit
+    loads[1].wait()
+    loads[2].wait()
     place = cluster_ref[...] * SPAN + order_ref[...]
     line_labels[0] = place
     column_labels[0] = place
@@ -185,13 +199,25 @@
 
     spread(0)
 
-    flat = [u for step in UNITS for u in step]
-    starts = [sum(len(s) for s in UNITS[:n]) // GROUP for n in range(STEPS + 1)]
+    lists = [part for both in UNITS for part in both]
+    flat = [u for part in lists for u in part]
+    starts = [sum(len(part) for part in lists[:m]) // GROUP for m in range(len(lists) + 1)]
     words = []
     for i in range(0, len(flat), GROUP):
         words.append(sum((r * 16 + g) << (7 * j) for j, (r, g) in enumerate(flat[i : i + GROUP])))
 
-    def step(n, before):
+    def line_answer(r):
+        return remote(
+            line_answers.at[r], line_got.at[r], line_answer_sent.at[r], line_answer_got.at[r],
+            relative(0, 0, LINES[r], 0),
+        )
+
+    def answer_line(r):
+        line_answers[r] = jnp.max(line_best[r].T, axis=0, keepdims=True)
+        if r:
+            line_answer(r).start()
+
+    def arrivals(n):
         k, h = n // 2, n % 2
         up(n).wait_recv()
         down(n).wait_recv()
@@ -201,40 +227,23 @@
             up(n + 2).start()
             down(n + 2).start()
 
-        @pl.when(h == 0)
-        def _():
-            up_label(k).wait_recv()
-
-            @pl.when(k < 3)
-            def _():
-                up_label(k + 1).start()
-                down_label(k).wait_recv()
-
-            @pl.when(k < 2)
-            def _():
-                down_label(k + 1).start()
-
         for at in (0, 2, 4):
             landing = [j for j in range(1, len(PLANE)) if LANDS[j] == at]
+            onward = [j for j in range(1, len(PLANE)) if LANDS[j] == at + 2]
 
             @pl.when((n == at) | (n == at + 1))
             def _():
                 for j in landing:
                     plane(j, h).wait_recv()
-                for j in range(1, len(PLANE)):
-                    if LANDS[j] == at + 2:
-                        plane(j, h).start()
+                for j in onward:
+                    plane(j, h).start()
 
             @pl.when(n == at)
             def _():
                 for j in landing:
                     plane_label(j).wait_recv()
-                for j in range(1, len(PLANE)):
-                    if LANDS[j] == at + 2:
-                        plane_label(j).start()
-                for j in [0] if at == 0 else [j for j in range(1, len(PLANE)) if LANDS[j] == at - 2]:
-                    across(j).wait_recv()
-                    across_label(j).wait_recv()
+                for j in onward:
+                    plane_label(j).start()
 
             @pl.when(n == at + 1)
             def _():
@@ -242,19 +251,48 @@
                     across(j).start()
                     across_label(j).start()
 
+        @pl.when(h == 0)
+        def _():
+            up_label(k).wait_recv()
+
+            @pl.when(k < 3)
+            def _():
+                up_label(k + 1).start()
+                down_label(k).wait_recv()
+
+            @pl.when(k < 2)
+            def _():
+                down_label(k + 1).start()
+
         @pl.when(n == 6)
         def _():
-            for j in range(1, len(PLANE)):
-                if LANDS[j] == 4:
-                    across(j).wait_recv()
-                    across_label(j).wait_recv()
-
             spread(7)
 
         @pl.when(h == 1)
         def _():
             spread(2 * k + 1)
             spread(2 * k + 2)
+
+    def from_sibling(n):
+        for at in (0, 1, 3, 5):
+
+            @pl.when(n == at)
+            def _():
+                for j in range(len(PLANE)):
+                    if (LANDS[j] + 1 if j else 0) == at:
+                        across(j).wait_recv()
+                        across_label(j).wait_recv()
+
+    def step(m, before):
+        n = m // 2
+
+        @pl.when(m % 2 == 0)
+        def _():
+            arrivals(n)
+
+        @pl.when(m % 2 == 1)
+        def _():
+            from_sibling(n)
 
         def group(u, carry):
             last_r, last_c = carry
@@ -269,9 +307,9 @@
                 last_r, last_c = r, 2 * g + 1
             return last_r, last_c
 
-        return lax.fori_loop(pick(starts, n), pick(starts[1:], n), group, before)
-
-    last_r, last_c = lax.fori_loop(0, STEPS, step, (jnp.int32(0), jnp.int32(0)))
+        return lax.fori_loop(pick(starts, m), pick(starts[1:], m), group, before)
+
+    last_r, last_c = lax.fori_loop(0, len(lists), step, (jnp.int32(0), jnp.int32(0)))
     keep_best(odd, last_r, last_c, column_labels, line_place, line_order, line_best, column_best)
 
     def column_best_of(c):
@@ -282,12 +320,6 @@
     to_sibling = remote(other_answers, sibling_in, sibling_sent, sibling_got, relative(0, 0, 0, 1))
     to_sibling.start()
 
-    def line_answer(r):
-        return remote(
-            line_answers.at[r], line_got.at[r], line_answer_sent.at[r], line_answer_got.at[r],
-            relative(0, 0, LINES[r], 0),
-        )
-
     def plane_answer(g):
         return remote(
             same_answers.at[g], column_got.at[g], plane_answer_sent.at[g], plane_answer_got.at[g],
@@ -295,9 +327,7 @@
         )
 
     for r in range(8):
-        line_answers[r] = jnp.max(line_best[r].T, axis=0, keepdims=True)
-        if r:
-            line_answer(r).start()
+        answer_line(r)
     to_sibling.wait_recv()
     for g in range(len(PLANE)):
         same_answers[g] = jnp.maximum(column_best_of(2 * g), sibling_in[g])
@@ -339,9 +369,13 @@
     best = pl.pallas_call(
         kernel,
         out_shape=jax.ShapeDtypeStruct((1, rows), jnp.float32),
-        in_specs=[pl.BlockSpec(memory_space=pltpu.VMEM)] * 3,
+        in_specs=[pl.BlockSpec(memory_space=pltpu.HBM)] * 3,
         out_specs=pl.BlockSpec(memory_space=pltpu.VMEM),
         scratch_shapes=[
+            pltpu.VMEM((rows, features), jnp.bfloat16),
+            pltpu.VMEM((1, rows), jnp.int32),
+            pltpu.VMEM((1, rows), jnp.int32),
+            dma((3,)),
             pltpu.VMEM((8, rows, features), jnp.bfloat16),
             pltpu.VMEM((2 * plane, rows, features), jnp.bfloat16),
             pltpu.VMEM((8, 1, rows), jnp.int32),

time: 60.6 us -> 59.1 us (0.975)
  Pallas kernels: 58.2 us -> 56.7 us
    pallas_call x1, Pallas kernels: 58.2 us -> 56.7 us  [on_device(): pl.pallas_call(kernel, out_shape=jax.ShapeDtypeStruct((1, rows), jnp.floa...]
where the time goes in v3:
time: 59.1 us; the launch traced here: 58.9 us
  Pallas kernels  56.7 us (96%)
  local copies, waits for them, and re-layouts  2.25 us (4%)
    pallas_call x1, Pallas kernels, on_device(): pl.pallas_call(kernel, out_shape=jax.ShapeDtypeStruct((1, rows), jnp.floa...  56.7 us
    unnamed x7, local copies, waits for them, and re-layouts  2.25 us

profile of v3, /device:TPU:1, one launch (start us, length us, event | category | flops | bytes accessed | tf_op | source)
XLA Modules:
  0.0 58.9 jit_solution(12037785086008085563)
XLA Ops:
  0.0 0.0 copy-start.2
  0.0 0.0 copy-start.1
  0.0 0.7 %copy-done.2 = s32[256]{0:T(256)S(1)} copy-done((s32[256]{0:T(256)S(1)}, s32[256]{0:T(256)}, u32[]{:S(2)}) %copy-start.2) | copy-done | bytes 1048
  0.7 0.0 copy-done.1
  0.7 0.0 copy-start
  0.7 1.0 %copy-done = bf16[256,768]{1,0:T(8,128)(2,1)S(1)} copy-done((bf16[256,768]{1,0:T(8,128)(2,1)S(1)}, bf16[256,768]{1,0:T(8,128)(2,1)}, u32[]{:S(2)}) %copy-start) | copy-done | bytes 393240
  1.7 56.7 %shard_map.37 = f32[1,256]{1,0:T(1,128)S(1)} custom-call(bf16[256,768]{1,0:T(8,128)(2,1)S(1)} %copy-done, s32[1,256]{1,0:T(1,128)S(1)} %bitcast.4, s32[1,256]{1,0:T(1,128)S(1)} %bitcast.5), custom_call_target="tpu_custom_call" | custom-call | flops 13690208256 | bytes 393216 | tf_op jit(solution)/shard_map/pallas_call | solution.py:369
  58.4 0.6 copy.5
Async XLA Ops:
  0.0 0.7 %copy-start.2 = (s32[256]{0:T(256)S(1)}, s32[256]{0:T(256)}, u32[]{:S(2)}) copy-start(s32[256]{0:T(256)} %param.5) | copy-start | bytes 3076
  0.0 0.7 %copy-start.1 = (s32[256,1]{0,1:T(1,128)S(1)}, s32[256,1]{0,1:T(1,128)}, u32[]{:S(2)}) copy-start(s32[256,1]{0,1:T(1,128)} %param.4) | copy-start | bytes 3076
  0.7 1.0 %copy-start = (bf16[256,768]{1,0:T(8,128)(2,1)S(1)}, bf16[256,768]{1,0:T(8,128)(2,1)}, u32[]{:S(2)}) copy-start(bf16[256,768]{1,0:T(8,128)(2,1)} %rows_hbm.1) | copy-start | bytes 1179652

commit v4 on v3

--- a/solution.py
+++ b/solution.py
@@ -9,25 +9,27 @@
 LINES = (0, 1, 7, 2, 6, 3, 5, 4)
 SOURCE = (None, 0, 0, 0, 1, 2, 3, 3, 6, 1)
 LANDS = (None, 0, 0, 0, 2, 2, 2, 2, 4, 4)
-GROUP = 4
-UNITS = (
-    ([], []),
-    ([], [(r, g) for r in (0, 1) for g in range(4)]),
-    ([], []),
-    (
-        [(2, g) for g in (1, 2, 3)] + [(3, g) for g in range(4)] + [(4, 1)],
-        [(4, 2), (4, 3), (2, 6), (2, 7)] + [(0, g) for g in (4, 5, 6, 7)],
-    ),
-    ([(r, g) for r in (1, 3) for g in (4, 5, 6, 7)], []),
-    (
-        [(4, 6), (4, 7)] + [(5, g) for g in range(8)] + [(6, 1), (6, 2)],
-        [(6, 3), (6, 6), (6, 7)] + [(r, g) for r in (0, 1, 3, 5) for g in (8, 9)] + [(2, 9)],
-    ),
-    ([(4, 9), (6, 9), (7, 0), (7, 1)], [(7, g) for g in range(2, 10)]),
+
+
+def both(*units):
+    return [(r, 2 * g + c, 0) for r, g in units for c in (0, 1)]
+
+
+BY_Z, BY_X, BY_Y = 1, 2, 3
+GROUP = 8
+TILES = (
+    [(0, 1, 0)] + both(*((0, g) for g in (1, 2, 3)), *((1, g) for g in range(4)), (2, 1), (2, 2), (2, 3))
+    + both(*((3, g) for g in range(4)), *((4, g) for g in (1, 2, 3)))
+    + [(0, 8, BY_X), (0, 10, BY_Y)] + both((2, 6), (2, 7), (0, 6), (0, 7), *((1, g) for g in (4, 5, 6, 7)))
+    + both(*((3, g) for g in (4, 5, 6, 7)), (4, 6), (4, 7))
+    + both(*((5, g) for g in range(8)), *((6, g) for g in (1, 2, 3, 6, 7)))
+    + [(0, 16, BY_X)] + both((0, 9), *((r, g) for r in (1, 3, 5) for g in (8, 9)), (2, 9), (4, 9), (6, 9))
+    + both(*((7, g) for g in (1, 2, 3, 6, 7, 9))) + [(7, 2 * g, BY_Z) for g in (0, 4, 5, 8)]
 )
-STEPS = len(UNITS)
+GROUPS = ((0, 0), (0, 2), (0, 0), (2, 2), (2, 0), (3, 3), (2, 0))
+STEPS = len(GROUPS)
 MESH = pl.DeviceIdType.MESH
-LOWEST = -(2**31)
+LOWEST, HIGHEST = -(2**31), 2**31 - 1
 SPAN = 65536
 
 
@@ -55,16 +57,15 @@
     )
 
 
-def keep_best(s, r, c, column_labels, line_place, line_order, line_best, column_best):
+def keep_best(s, r, c, column_labels, line_place, line_order, line_best, column_best, same_rows=False):
     label = column_labels[c]
     wide = []
     for left in (0, 128):
         p = label[:, left : left + 128]
         wide.append(
             [
-                jnp.broadcast_to(p + (LOWEST + 1), (8, 128)),
-                jnp.broadcast_to(p + LOWEST - 1, (8, 128)),
-                jnp.broadcast_to((p & (SPAN - 1)) + LOWEST, (8, 128)),
+                jnp.broadcast_to(p + LOWEST, (8, 128)),
+                jnp.broadcast_to(HIGHEST - (p & (SPAN - 1)), (8, 128)),
                 jnp.full((8, 128), -1.0, jnp.float32),
             ]
         )
@@ -72,14 +73,18 @@
         mine, order = line_place[r, top : top + 8, :], line_order[r, top : top + 8, :]
         best = line_best[r, top : top + 8, :]
         for i, left in enumerate((0, 128)):
-            after, before, other_order, down = wide[i]
+            theirs, limit, down = wide[i]
+            ahead = mine - theirs
             v = s[top : top + 8, left : left + 128]
-            best = jnp.maximum(best, jnp.where(mine - after < order, v, -1.0))
-            wide[i][3] = jnp.maximum(down, jnp.where(before - mine < other_order, v, -1.0))
+            earlier = ahead <= order
+            if same_rows:
+                earlier &= ahead != LOWEST
+            best = jnp.maximum(best, jnp.where(earlier, v, -1.0))
+            wide[i][2] = jnp.maximum(down, jnp.where(ahead > limit, v, -1.0))
         line_best[r, top : top + 8, :] = best
     for i, left in enumerate((0, 128)):
         here = column_best.at[c, :, pl.ds(left, 128)]
-        here[...] = jnp.maximum(here[...], wide[i][3])
+        here[...] = jnp.maximum(here[...], wide[i][2])
 
 
 def kernel(
@@ -173,16 +178,16 @@
             across_label_sent.at[k], across_label_got.at[k], relative(0, 0, 0, 1),
         )
 
-    first = [k for k in range(1, len(PLANE)) if LANDS[k] == 0]
+    near = [k for k in range(1, len(PLANE)) if LANDS[k] == 0]
     for h in (0, 1):
         up(jnp.int32(h)).start()
         down(jnp.int32(h)).start()
-        for k in first:
+        for k in near:
             plane(k, h).start()
         if h == 0:
             up_label(jnp.int32(0)).start()
             down_label(jnp.int32(0)).start()
-            for k in first:
+            for k in near:
                 plane_label(k).start()
     across(0).start()
     across_label(0).start()
@@ -198,13 +203,18 @@
             line_order[r, top : top + 128, :] = (column & (SPAN - 1)) + LOWEST
 
     spread(0)
-
-    lists = [part for both in UNITS for part in both]
-    flat = [u for part in lists for u in part]
-    starts = [sum(len(part) for part in lists[:m]) // GROUP for m in range(len(lists) + 1)]
-    words = []
-    for i in range(0, len(flat), GROUP):
-        words.append(sum((r * 16 + g) << (7 * j) for j, (r, g) in enumerate(flat[i : i + GROUP])))
+    even[...] = scores(lines, 0, columns, 0)
+    keep_best(even, 0, 0, column_labels, line_place, line_order, line_best, column_best, same_rows=True)
+
+    counts = [count for step in GROUPS for count in step]
+    starts = [sum(counts[:m]) for m in range(len(counts) + 1)]
+    coded = [r * 128 + c * 4 + bit for r, c, bit in TILES]
+    words = [
+        [sum(t << (10 * j) for j, t in enumerate(coded[i + first : min(i + first + 3, i + GROUP)])) for i in range(0, len(coded), GROUP)]
+        for first in range(0, GROUP, 3)
+    ]
+    x, y, z, _ = whereabouts()
+    bits = z // 4 * 2 + x // 2 * 4 + y // 2 * 8
 
     def line_answer(r):
         return remote(
@@ -296,20 +306,20 @@
 
         def group(u, carry):
             last_r, last_c = carry
-            word = pick(words, u)
+            held = [pick(word, u) for word in words]
             for i in range(GROUP):
-                code = (word >> (7 * i)) & 127
-                r, g = code >> 4, code & 15
-                even[...] = scores(lines, r, columns, 2 * g)
-                keep_best(odd, last_r, last_c, column_labels, line_place, line_order, line_best, column_best)
-                odd[...] = scores(lines, r, columns, 2 * g + 1)
-                keep_best(even, r, 2 * g, column_labels, line_place, line_order, line_best, column_best)
-                last_r, last_c = r, 2 * g + 1
+                code = (held[i // 3] >> (10 * (i % 3))) & 1023
+                r = code >> 7
+                c = ((code >> 2) & 31) + ((bits >> (code & 3)) & 1)
+                now, then = (even, odd) if i % 2 == 0 else (odd, even)
+                now[...] = scores(lines, r, columns, c)
+                keep_best(then, last_r, last_c, column_labels, line_place, line_order, line_best, column_best)
+                last_r, last_c = r, c
             return last_r, last_c
 
         return lax.fori_loop(pick(starts, m), pick(starts[1:], m), group, before)
 
-    last_r, last_c = lax.fori_loop(0, len(lists), step, (jnp.int32(0), jnp.int32(0)))
+    last_r, last_c = lax.fori_loop(0, len(counts), step, (jnp.int32(0), jnp.int32(0)))
     keep_best(odd, last_r, last_c, column_labels, line_place, line_order, line_best, column_best)
 
     def column_best_of(c):

time: 59.1 us -> 58.5 us (0.990)
  Pallas kernels: 56.7 us -> 56.1 us
where the time goes in v4:
time: 58.5 us; the launch traced here: 58.4 us
  Pallas kernels  56.1 us (96%)
  local copies, waits for them, and re-layouts  2.25 us (4%)
    pallas_call x1, Pallas kernels, on_device(): pl.pallas_call(kernel, out_shape=jax.ShapeDtypeStruct((1, rows), jnp.floa...  56.1 us
    unnamed x7, local copies, waits for them, and re-layouts  2.25 us

profile of v4, /device:TPU:1, one launch (start us, length us, event | category | flops | bytes accessed | tf_op | source)
XLA Modules:
  0.0 58.4 jit_solution(9019557698007573379)
XLA Ops:
  0.0 0.0 copy-start.2
  0.0 0.0 copy-start.1
  0.0 0.7 %copy-done.2 = s32[256]{0:T(256)S(1)} copy-done((s32[256]{0:T(256)S(1)}, s32[256]{0:T(256)}, u32[]{:S(2)}) %copy-start.2) | copy-done | bytes 1048
  0.7 0.0 copy-done.1
  0.7 0.0 copy-start
  0.7 1.0 %copy-done = bf16[256,768]{1,0:T(8,128)(2,1)S(1)} copy-done((bf16[256,768]{1,0:T(8,128)(2,1)S(1)}, bf16[256,768]{1,0:T(8,128)(2,1)}, u32[]{:S(2)}) %copy-start) | copy-done | bytes 393240
  1.7 56.1 %shard_map.37 = f32[1,256]{1,0:T(1,128)S(1)} custom-call(bf16[256,768]{1,0:T(8,128)(2,1)S(1)} %copy-done, s32[1,256]{1,0:T(1,128)S(1)} %bitcast.4, s32[1,256]{1,0:T(1,128)S(1)} %bitcast.5), custom_call_target="tpu_custom_call" | custom-call | flops 13690208256 | bytes 393216 | tf_op jit(solution)/shard_map/pallas_call | solution.py:379
  57.8 0.6 copy.5
Async XLA Ops:
  0.0 0.7 %copy-start.2 = (s32[256]{0:T(256)S(1)}, s32[256]{0:T(256)}, u32[]{:S(2)}) copy-start(s32[256]{0:T(256)} %param.5) | copy-start | bytes 3076
  0.0 0.7 %copy-start.1 = (s32[256,1]{0,1:T(1,128)S(1)}, s32[256,1]{0,1:T(1,128)}, u32[]{:S(2)}) copy-start(s32[256,1]{0,1:T(1,128)} %param.4) | copy-start | bytes 3076
  0.7 1.0 %copy-start = (bf16[256,768]{1,0:T(8,128)(2,1)S(1)}, bf16[256,768]{1,0:T(8,128)(2,1)}, u32[]{:S(2)}) copy-start(bf16[256,768]{1,0:T(8,128)(2,1)} %rows_hbm.1) | copy-start | bytes 1179652

commit v5 on v4

--- a/solution.py
+++ b/solution.py
@@ -23,10 +23,10 @@
     + [(0, 8, BY_X), (0, 10, BY_Y)] + both((2, 6), (2, 7), (0, 6), (0, 7), *((1, g) for g in (4, 5, 6, 7)))
     + both(*((3, g) for g in (4, 5, 6, 7)), (4, 6), (4, 7))
     + both(*((5, g) for g in range(8)), *((6, g) for g in (1, 2, 3, 6, 7)))
-    + [(0, 16, BY_X)] + both((0, 9), *((r, g) for r in (1, 3, 5) for g in (8, 9)), (2, 9), (4, 9), (6, 9))
-    + both(*((7, g) for g in (1, 2, 3, 6, 7, 9))) + [(7, 2 * g, BY_Z) for g in (0, 4, 5, 8)]
+    + both(*((7, g) for g in (1, 2, 3, 6, 7))) + [(7, 2 * g, BY_Z) for g in (0, 4, 5)]
+    + [(0, 16, BY_X), (7, 16, BY_Z)] + both(*((r, 8) for r in (1, 3, 5)), *((r, 9) for r in range(8)))
 )
-GROUPS = ((0, 0), (0, 2), (0, 0), (2, 2), (2, 0), (3, 3), (2, 0))
+GROUPS = ((0, 0), (0, 2), (0, 0), (2, 2), (2, 0), (3, 0), (2, 3))
 STEPS = len(GROUPS)
 MESH = pl.DeviceIdType.MESH
 LOWEST, HIGHEST = -(2**31), 2**31 - 1
@@ -241,7 +241,7 @@
             landing = [j for j in range(1, len(PLANE)) if LANDS[j] == at]
             onward = [j for j in range(1, len(PLANE)) if LANDS[j] == at + 2]
 
-            @pl.when((n == at) | (n == at + 1))
+            @pl.when((n == at) | ((n == at + 1) & (at < 4)))
             def _():
                 for j in landing:
                     plane(j, h).wait_recv()
@@ -255,7 +255,7 @@
                 for j in onward:
                     plane_label(j).start()
 
-            @pl.when(n == at + 1)
+            @pl.when((n == at + 1) & (at < 4))
             def _():
                 for j in landing:
                     across(j).start()
@@ -284,12 +284,21 @@
             spread(2 * k + 2)
 
     def from_sibling(n):
-        for at in (0, 1, 3, 5):
+        last = [j for j in range(1, len(PLANE)) if LANDS[j] == 4]
+
+        @pl.when(n == 5)
+        def _():
+            for j in last:
+                plane(j, 1).wait_recv()
+                across(j).start()
+                across_label(j).start()
+
+        for at in (0, 1, 3, 6):
 
             @pl.when(n == at)
             def _():
                 for j in range(len(PLANE)):
-                    if (LANDS[j] + 1 if j else 0) == at:
+                    if (0 if j == 0 else 6 if j in last else LANDS[j] + 1) == at:
                         across(j).wait_recv()
                         across_label(j).wait_recv()
 

time: 58.5 us -> 58.6 us (level)
  no operation moved by 1% of the time
where the time goes in v5:
time: 58.6 us; the launch traced here: 58.5 us
  Pallas kernels  56.2 us (96%)
  local copies, waits for them, and re-layouts  2.25 us (4%)
    pallas_call x1, Pallas kernels, on_device(): pl.pallas_call(kernel, out_shape=jax.ShapeDtypeStruct((1, rows), jnp.floa...  56.2 us
    unnamed x7, local copies, waits for them, and re-layouts  2.25 us

profile of v5, /device:TPU:1, one launch (start us, length us, event | category | flops | bytes accessed | tf_op | source)
XLA Modules:
  0.0 58.5 jit_solution(3651453162155497922)
XLA Ops:
  0.0 0.0 copy-start.2
  0.0 0.0 copy-start.1
  0.0 0.7 %copy-done.2 = s32[256]{0:T(256)S(1)} copy-done((s32[256]{0:T(256)S(1)}, s32[256]{0:T(256)}, u32[]{:S(2)}) %copy-start.2) | copy-done | bytes 1048
  0.7 0.0 copy-done.1
  0.7 0.0 copy-start
  0.7 1.0 %copy-done = bf16[256,768]{1,0:T(8,128)(2,1)S(1)} copy-done((bf16[256,768]{1,0:T(8,128)(2,1)S(1)}, bf16[256,768]{1,0:T(8,128)(2,1)}, u32[]{:S(2)}) %copy-start) | copy-done | bytes 393240
  1.7 56.2 %shard_map.37 = f32[1,256]{1,0:T(1,128)S(1)} custom-call(bf16[256,768]{1,0:T(8,128)(2,1)S(1)} %copy-done, s32[1,256]{1,0:T(1,128)S(1)} %bitcast.4, s32[1,256]{1,0:T(1,128)S(1)} %bitcast.5), custom_call_target="tpu_custom_call" | custom-call | flops 13690208256 | bytes 393216 | tf_op jit(solution)/shard_map/pallas_call | solution.py:388
  57.9 0.6 copy.5
Async XLA Ops:
  0.0 0.7 %copy-start.2 = (s32[256]{0:T(256)S(1)}, s32[256]{0:T(256)}, u32[]{:S(2)}) copy-start(s32[256]{0:T(256)} %param.5) | copy-start | bytes 3076
  0.0 0.7 %copy-start.1 = (s32[256,1]{0,1:T(1,128)S(1)}, s32[256,1]{0,1:T(1,128)}, u32[]{:S(2)}) copy-start(s32[256,1]{0,1:T(1,128)} %param.4) | copy-start | bytes 3076
  0.7 1.0 %copy-start = (bf16[256,768]{1,0:T(8,128)(2,1)S(1)}, bf16[256,768]{1,0:T(8,128)(2,1)}, u32[]{:S(2)}) copy-start(bf16[256,768]{1,0:T(8,128)(2,1)} %rows_hbm.1) | copy-start | bytes 1179652

commit v6 on v5

--- a/solution.py
+++ b/solution.py
@@ -88,7 +88,7 @@
 
 
 def kernel(
-    rows_hbm, cluster_hbm, order_hbm, out_ref, rows_ref, cluster_ref, order_ref, loaded,
+    rows_ref, cluster_ref, order_ref, out_ref,
     lines, columns, line_labels, column_labels, line_place, line_order, line_best, column_best, even, odd,
     line_answers, same_answers, other_answers, sibling_in, line_got, column_got,
     up_sent, up_got, down_sent, down_got, line_label_sent, line_label_got,
@@ -99,12 +99,6 @@
     def remote(src, dst, sent, got, device):
         return pltpu.make_async_remote_copy(src, dst, sent, got, device_id=device, device_id_type=MESH)
 
-    loads = [
-        pltpu.make_async_copy(src, dst, loaded.at[i])
-        for i, (src, dst) in enumerate(((rows_hbm, rows_ref), (cluster_hbm, cluster_ref), (order_hbm, order_ref)))
-    ]
-    for load in loads:
-        load.start()
     barrier = pltpu.get_barrier_semaphore()
     hello = {(0, 0, 1, 0), (0, 0, 7, 0), (0, 0, 0, 1)}
     for k in range(1, len(PLANE)):
@@ -113,15 +107,12 @@
     for offset in sorted(hello):
         pl.semaphore_signal(barrier, inc=1, device_id=relative(*offset), device_id_type=MESH)
 
-    loads[0].wait()
     for top in range(0, 256, 32):
         wide = rows_ref[top : top + 32, :].astype(jnp.float32)
         scale = lax.rsqrt(jnp.sum(wide * wide, axis=1, keepdims=True) + 1e-06)
         unit = (wide * scale).astype(jnp.bfloat16)
         lines[0, top : top + 32, :] = unit
         columns[0, top : top + 32, :] = unit
-    loads[1].wait()
-    loads[2].wait()
     place = cluster_ref[...] * SPAN + order_ref[...]
     line_labels[0] = place
     column_labels[0] = place
@@ -388,13 +379,9 @@
     best = pl.pallas_call(
         kernel,
         out_shape=jax.ShapeDtypeStruct((1, rows), jnp.float32),
-        in_specs=[pl.BlockSpec(memory_space=pltpu.HBM)] * 3,
+        in_specs=[pl.BlockSpec(memory_space=pltpu.VMEM)] * 3,
         out_specs=pl.BlockSpec(memory_space=pltpu.VMEM),
         scratch_shapes=[
-            pltpu.VMEM((rows, features), jnp.bfloat16),
-            pltpu.VMEM((1, rows), jnp.int32),
-            pltpu.VMEM((1, rows), jnp.int32),
-            dma((3,)),
             pltpu.VMEM((8, rows, features), jnp.bfloat16),
             pltpu.VMEM((2 * plane, rows, features), jnp.bfloat16),
             pltpu.VMEM((8, 1, rows), jnp.int32),

time: 58.6 us -> 58.5 us (level)
  no operation moved by 1% of the time
where the time goes in v6:
time: 58.5 us; the launch traced here: 58.4 us
  Pallas kernels  56.1 us (96%)
  local copies, waits for them, and re-layouts  2.25 us (4%)
    pallas_call x1, Pallas kernels, on_device(): pl.pallas_call(kernel, out_shape=jax.ShapeDtypeStruct((1, rows), jnp.floa...  56.1 us
    unnamed x7, local copies, waits for them, and re-layouts  2.25 us

profile of v6, /device:TPU:1, one launch (start us, length us, event | category | flops | bytes accessed | tf_op | source)
XLA Modules:
  0.0 58.4 jit_solution(3570057691701518282)
XLA Ops:
  0.0 0.0 copy-start.2
  0.0 0.0 copy-start.1
  0.0 0.7 %copy-done.2 = s32[256]{0:T(256)S(1)} copy-done((s32[256]{0:T(256)S(1)}, s32[256]{0:T(256)}, u32[]{:S(2)}) %copy-start.2) | copy-done | bytes 1048
  0.7 0.0 copy-done.1
  0.7 0.0 copy-start
  0.7 1.0 %copy-done = bf16[256,768]{1,0:T(8,128)(2,1)S(1)} copy-done((bf16[256,768]{1,0:T(8,128)(2,1)S(1)}, bf16[256,768]{1,0:T(8,128)(2,1)}, u32[]{:S(2)}) %copy-start) | copy-done | bytes 393240
  1.7 56.1 %shard_map.37 = f32[1,256]{1,0:T(1,128)S(1)} custom-call(bf16[256,768]{1,0:T(8,128)(2,1)S(1)} %copy-done, s32[1,256]{1,0:T(1,128)S(1)} %bitcast.4, s32[1,256]{1,0:T(1,128)S(1)} %bitcast.5), custom_call_target="tpu_custom_call" | custom-call | flops 13690208256 | bytes 393216 | tf_op jit(solution)/shard_map/pallas_call | solution.py:379
  57.8 0.6 copy.5
Async XLA Ops:
  0.0 0.7 %copy-start.2 = (s32[256]{0:T(256)S(1)}, s32[256]{0:T(256)}, u32[]{:S(2)}) copy-start(s32[256]{0:T(256)} %param.5) | copy-start | bytes 3076
  0.0 0.7 %copy-start.1 = (s32[256,1]{0,1:T(1,128)S(1)}, s32[256,1]{0,1:T(1,128)}, u32[]{:S(2)}) copy-start(s32[256,1]{0,1:T(1,128)} %param.4) | copy-start | bytes 3076
  0.7 1.0 %copy-start = (bf16[256,768]{1,0:T(8,128)(2,1)S(1)}, bf16[256,768]{1,0:T(8,128)(2,1)}, u32[]{:S(2)}) copy-start(bf16[256,768]{1,0:T(8,128)(2,1)} %rows_ref.1) | copy-start | bytes 1179652
